TPU v7x, 256 devices: a whole 4x4x8 slice. The times are simulated.
256 devices in a mesh: exp: 4 (over z_lo), inner: 4 (over z_hi, core), outer: 16 (over x, y).
Axes of the slice: x: 4, y: 4, z: 8 (z_hi: 2, z_lo: 4; z = z_hi * 4 + z_lo), core: 2. Of those that a mesh axis runs over, the one named last changes fastest.
Arguments:
- activations: bfloat16 [262144, 2048], P(('exp', 'inner', 'outer')), parts along dimension 0, may hold values from -6 to 6
- cotangent: bfloat16 [262144, 768], P(('exp', 'inner', 'outer')), parts along dimension 0, may hold values from -0.0625 to 0.0625
- tile_rows: int32 [2048], P(('exp', 'inner', 'outer')), parts along dimension 0, may hold values from 1 to 128, as said below
- params: bfloat16 [8192, 768], P(('exp', 'inner')), parts along dimension 0, may hold values from -5 to 5
- first_moment: float32 [8192, 768], P(('exp', 'inner')), parts along dimension 0, may hold values from -0.6 to 0.6
- second_moment: float32 [8192, 768], P(('exp', 'inner')), parts along dimension 0, may hold values from 0.005 to 0.05
Outputs:
- new_params: bfloat16 [8192, 768], P('exp'), parts along dimension 0
- first_new: float32 [8192, 768], P(('exp', 'inner', 'outer')), parts along dimension 0
- second_new: float32 [8192, 768], P(('exp', 'inner', 'outer')), parts along dimension 0
There are 4 independent parts, one for each index of `exp`. A program takes and returns all parts, laid end to end along the dimension named above; each array names one. Nothing has to cross between parts.
Inputs may be any that keep to these rules, and one draw needn't show every extreme that they name: In each tile the live rows are the first tile_rows[t] rows.
All inputs are finite; a program needn't handle non-finite values.
Results may differ from a plain program's by a relative error of at most 0.001.
Values may be sent and summed in bfloat16 or wider, within the bound.
A program may use at most 64 MiB of HBM per device.

v0:
```python
import jax
import jax.numpy as jnp
from jax import lax
from jax.sharding import PartitionSpec as P

beta_one = 0.9
beta_two = 0.95
learn_rate = 0.05
weight_decay = 0.1
epsilon = 1e-08


def adamw(grad, params, first_moment, second_moment):
    first_new = beta_one * first_moment + (1.0 - beta_one) * grad
    second_new = beta_two * second_moment + (1.0 - beta_two) * grad * grad
    update = (
        first_new / (1.0 - beta_one**3) / (jnp.sqrt(second_new / (1.0 - beta_two**3)) + epsilon)
    )
    weights = params.astype(jnp.float32)
    new_params = (weights - learn_rate * (update + weight_decay * weights)).astype(jnp.bfloat16)
    return (new_params, first_new, second_new)


def take_rows(array, start, count):
    return lax.dynamic_slice_in_dim(array, start, count, 0)


def shards(activations, cotangent, tile_rows, params, first_moment, second_moment):
    rows = activations.shape[0]
    tiles = tile_rows.shape[0]
    within = lax.broadcasted_iota(jnp.int32, (tiles, rows // tiles), 1)
    live = (within < tile_rows[:, None]).reshape(rows, 1)
    masked = jnp.where(live, cotangent, jnp.zeros_like(cotangent))
    shard_rows = params.shape[0]
    piece_rows = shard_rows // lax.axis_size("outer")
    offset = lax.axis_index("outer") * piece_rows
    partial_grad = lax.psum_scatter(
        lax.dot_general(
            activations, masked, (((0,), (0,)), ((), ())), preferred_element_type=jnp.float32
        ),
        "inner",
        scatter_dimension=0,
        tiled=True,
    )
    grad = lax.psum(partial_grad, "outer")
    row_shard, first_new, second_new = adamw(grad, params, first_moment, second_moment)
    whole = lax.all_gather(row_shard, "inner", axis=0, tiled=True)
    return (
        whole,
        take_rows(first_new, offset, piece_rows),
        take_rows(second_new, offset, piece_rows),
    )


def solution(mesh):
    in_specs = (
        P(("exp", "inner", "outer"), None),
        P(("exp", "inner", "outer"), None),
        P(("exp", "inner", "outer")),
        P(("exp", "inner"), None),
        P(("exp", "inner"), None),
        P(("exp", "inner"), None),
    )
    out_specs = (
        P("exp", None),
        P(("exp", "inner", "outer"), None),
        P(("exp", "inner", "outer"), None),
    )
    return jax.shard_map(shards, mesh=mesh, in_specs=in_specs, out_specs=out_specs, check_vma=False)
```

profile of v0, /device:TPU:1, one launch (start us, length us, event | category | flops | bytes accessed | tf_op | source)
XLA Modules:
  0.0 297.6 jit_solution(6954048550051688790)
XLA Ops:
  7.2 0.0 reduce-scatter.2.cloned.1.call-start
  7.2 0.7 fusion.7
  7.9 8.9 %convolution_bitcast_fusion = f32[2048,768]{0,1:T(8,128)} fusion(bf16[1024,2048]{1,0:T(8,128)(2,1)} %param.6, bf16[1024,768]{1,0:T(8,128)(2,1)} %param.7, pred[1024]{0:T(1024)(128)(4,1)S(1)} %fusion.7), kind=kOutput, calls=%fused_computation | convolution fusion | flops 3222011904 | bytes 12059648 | tf_op jit(solution)/shard_map/dot_general | solution.py:38
  16.8 0.0 reduce-scatter.2.cloned.1.call-update
  16.9 0.0 copy-start
  16.9 0.0 all-reduce.2.cloned.1.call-start
  16.9 111.3 %reduce-scatter.2.cloned.1.call-done = f32[512,768]{0,1:T(8,128)} async-done(((f32[2048,768]{0,1:T(8,128)}), f32[512,768]{0,1:T(8,128)}) %reduce-scatter.2.cloned.1.call-update) | async-done | bytes 1572880 | tf_op jit(solution)/shard_map/reduce_scatter | solution.py:37
  128.2 0.0 all-reduce.2.cloned.1.call-update
  128.2 0.0 all-gather.2.cloned.1.call-start
  128.2 0.0 copy-done
  128.3 0.5 copy.10
  128.7 1.9 copy.11
  130.6 2.3 copy.9
  132.9 92.5 %all-reduce.2.cloned.1.call-done = f32[512,768]{0,1:T(8,128)} async-done(((f32[512,768]{0,1:T(8,128)}), f32[512,768]{0,1:T(8,128)}) %all-reduce.2.cloned.1.call-update) | async-done | bytes 1572880 | tf_op jit(solution)/shard_map/psum | solution.py:45
  225.4 4.6 %fusion.2 = (bf16[512,768]{0,1:T(8,128)(2,1)}, f32[512,768]{0,1:T(8,128)}, f32[512,768]{0,1:T(8,128)}) fusion(bf16[512,768]{0,1:T(8,128)(2,1)} %copy.9, f32[512,768]{0,1:T(8,128)} %all-reduce.2.cloned.1.call-done, f32[512,768]{0,1:T(8,128)S(1)} %copy.10, f32[512,768]{0,1:T(8,128)S(1)} %copy.11), kind=kLoop, calls=%fused_computation.6 | loop fusion | flops 6684672 | bytes 9437184 | tf_op jit(solution)/shard_map/convert_element_type | solution.py:20
  230.1 0.0 all-gather.2.cloned.1.call-update
  230.1 1.4 constant_dynamic-slice_fusion
  231.5 0.8 copy.13
  232.3 0.8 copy.14
  233.1 53.3 %all-gather.2.cloned.1.call-done = bf16[2048,768]{0,1:T(8,128)(2,1)} async-done(((bf16[512,768]{0,1:T(8,128)(2,1)}), bf16[2048,768]{0,1:T(8,128)(2,1)}) %all-gather.2.cloned.1.call-update) | async-done | bytes 3145744 | tf_op jit(solution)/shard_map/all_gather | solution.py:47
  286.4 4.6 %copy.12 = bf16[2048,768]{1,0:T(8,128)(2,1)} copy(bf16[2048,768]{0,1:T(8,128)(2,1)} %all-gather.2.cloned.1.call-done) | data formatting | bytes 6291456
Async XLA Ops:
  7.2 121.0 %reduce-scatter.2.cloned.1.call-start = ((), (), s32[]{:S(2)}) async-start(), calls=%async_computation.1 | async-start | bytes 7864320 | tf_op jit(solution)/shard_map/reduce_scatter | solution.py:37
  16.9 111.4 %copy-start = (f32[512,768]{1,0:T(8,128)S(1)}, f32[512,768]{1,0:T(8,128)}, u32[]{:S(2)}) copy-start(f32[512,768]{1,0:T(8,128)} %param.10) | copy-start | bytes 4718596
  16.9 208.6 %all-reduce.2.cloned.1.call-start = ((), (), s32[]{:S(2)}) async-start(), calls=%async_computation.2 | async-start | bytes 3145728 | tf_op jit(solution)/shard_map/psum | solution.py:45
  128.2 158.2 %all-gather.2.cloned.1.call-start = ((), (), s32[]{:S(2)}) async-start(), calls=%async_computation.3 | async-start | bytes 3932160 | tf_op jit(solution)/shard_map/all_gather | solution.py:47
Sparse Core Ops, SparseCore 0:
  17.0 111.1 reduce-scatter.1
  131.8 93.5 all-reduce.1
  230.2 56.1 all-gather.1
where the time goes:
time: 298 us
  waiting for transfers between devices  257 us (86%)
  between operations  13.8 us (5%)
  local copies, waits for them, and re-layouts  12.3 us (4%)
  matrix products  8.89 us (3%)
  other arithmetic  5.37 us (2%)
    reduce_scatter x1, waiting for transfers between devices, shards(): lax.psum_scatter(lax.dot_general(activations, masked, (((0,), (0,)), ((),...  111 us
    psum x1, waiting for transfers between devices, shards(): grad = lax.psum(partial_grad, 'outer')  92.5 us
    all_gather x1, waiting for transfers between devices, shards(): whole = lax.all_gather(row_shard, 'inner', axis=0, tiled=True)  53.3 us
    unnamed x8, local copies, waits for them, and re-layouts  10.9 us
    dot_general x1, matrix products, shards(): lax.dot_general(activations, masked, (((0,), (0,)), ((), ())), preferred_...  8.89 us
  transfers between devices with their start and end apart: 3, of which 3 were waited for; matrix products, arithmetic and copies ran while one was open for 3% of the time, Pallas kernels for 0%

commit v1 on v0

v1 whole, which is shorter than its diff:
```python
import functools

import jax
import jax.numpy as jnp
from jax import lax
from jax.experimental import pallas as pl
from jax.experimental.pallas import tpu as pltpu
from jax.sharding import PartitionSpec as P

beta_one = 0.9
beta_two = 0.95
learn_rate = 0.05
weight_decay = 0.1
epsilon = 1e-08

MESH = pl.DeviceIdType.MESH
SIDE = 4
ROWS = 32
COLS = 768
HALF = 384
BLOCK = SIDE * SIDE * ROWS
LANES = 128
LEVELS = 32767.0
F32 = jnp.float32


def adamw(grad, params, first_moment, second_moment):
    first_new = beta_one * first_moment + (1.0 - beta_one) * grad
    second_new = beta_two * second_moment + (1.0 - beta_two) * grad * grad
    update = (
        first_new / (1.0 - beta_one**3) / (jnp.sqrt(second_new / (1.0 - beta_two**3)) + epsilon)
    )
    weights = params.astype(F32)
    new_params = (weights - learn_rate * (update + weight_decay * weights)).astype(jnp.bfloat16)
    return (new_params, first_new, second_new)


def spread(row, columns):
    return jnp.concatenate([row] * (columns // LANES), axis=1)


def encode(value, code_ref, scale_ref):
    columns = value.shape[1]
    top = jnp.max(jnp.abs(value), axis=0, keepdims=True)
    peak = top[:, :LANES]
    for at in range(LANES, columns, LANES):
        peak = jnp.maximum(peak, top[:, at : at + LANES])
    peak = jnp.maximum(peak, 1e-30)
    code = jnp.round(value * spread(LEVELS / peak, columns)).astype(jnp.int32)
    code_ref[...] = code.astype(jnp.int16).reshape(code_ref.shape)
    scale_ref[...] = jnp.broadcast_to(peak * (1.0 / LEVELS), scale_ref.shape)


def decode(code, scale_ref):
    columns = code.shape[-1]
    value = code.reshape(-1, columns).astype(jnp.int32).astype(F32)
    return value * spread(scale_ref[0:1, :], columns)


def kernel(
    acts, cot, tiles, params, first, second,
    out, first_out, second_out,
    act_buf, cot_buf, mask_buf, par_buf, mom_buf, acc, tmp,
    sib_code, sib_scale, one_code, one_scale, two_code, two_scale, z_code, z_scale,
    part, whole,
    load_sem, sib_sem, one_sem, two_sem, z_sem, far_sem, up_sem, over_sem, twin_sem,
):
    exp, inner, outer = lax.axis_index("exp"), lax.axis_index("inner"), lax.axis_index("outer")
    x, y = outer // SIDE, outer % SIDE
    plane, core = inner // 2, inner % 2
    other = 1 - plane

    twin = (exp, plane * 2 + 1 - core, outer)
    far = (exp, other * 2 + core, outer)

    def along(axis, step):
        if axis == 0:
            return (exp, inner, (x + step) % SIDE * SIDE + y)
        return (exp, inner, x * SIDE + (y + step) % SIDE)

    def column(block, who):
        return pl.multiple_of((block * 2 + who) * BLOCK, BLOCK)

    blocks = (other, plane)
    load_cot = pltpu.make_async_copy(cot, cot_buf, load_sem.at[0])
    load_cot.start()
    loads = []
    for b in range(2):
        for own in range(2):
            who = core if own else 1 - core
            load = pltpu.make_async_copy(
                acts.at[:, pl.ds(column(blocks[b], who), BLOCK)],
                act_buf.at[2 * b + own],
                load_sem.at[1 + 2 * b + own],
            )
            load.start()
            loads.append(load)
    mine = pl.ds(pl.multiple_of(outer * ROWS, ROWS), ROWS)
    state = [
        pltpu.make_async_copy(params.at[mine, :], par_buf, load_sem.at[5]),
        pltpu.make_async_copy(first.at[mine, :], mom_buf.at[0], load_sem.at[6]),
        pltpu.make_async_copy(second.at[mine, :], mom_buf.at[1], load_sem.at[7]),
    ]
    for load in state:
        load.start()

    barrier = pltpu.get_barrier_semaphore()
    partners = [twin, far] + [along(a, s) for a in range(2) for s in (1, 2, 3)]
    for partner in partners:
        pl.semaphore_signal(barrier, inc=1, device_id=partner, device_id_type=MESH)

    load_cot.wait()
    tile = cot_buf.shape[0] // tiles.shape[0]
    within = lax.broadcasted_iota(jnp.int32, (tile, COLS), 0)
    for t in range(tiles.shape[0]):
        rows = pl.ds(t * tile, tile)
        value = cot_buf[rows, :]
        mask_buf[rows, :] = jnp.where(within < tiles[t], value, jnp.zeros_like(value))

    started = []

    def send(src, dst, sems, device):
        copy = pltpu.make_async_remote_copy(
            src_ref=src, dst_ref=dst, send_sem=sems.at[0], recv_sem=sems.at[1],
            device_id=device, device_id_type=MESH,
        )
        copy.start()
        started.append(copy)
        return copy

    def send_coded(value, code, scale, sems, device):
        encode(value, code.at[0], scale.at[0])
        return (
            send(scale.at[0], scale.at[1], sems.at[1], device),
            send(code.at[0], code.at[1], sems.at[0], device),
        )

    def arrived(copies):
        for copy in copies:
            copy.wait_recv()

    def product(at):
        loads[at].wait()
        return lax.dot_general(
            act_buf[at], mask_buf[...], (((0,), (0,)), ((), ())), preferred_element_type=F32
        )

    def to_twin(b):
        tmp[...] = product(2 * b)
        if b == 0:
            pl.semaphore_wait(barrier, len(partners))
        return send_coded(tmp[...], sib_code.at[b], sib_scale.at[b], sib_sem.at[b], twin)

    def own(b):
        acc[b] = product(2 * b + 1).reshape(SIDE, SIDE, ROWS, COLS)

    def halves(b, axis, at):
        if axis == 0:
            return acc[b, at, :, :, :HALF].reshape(SIDE * ROWS, HALF)
        return acc[b, :, at, :, HALF:].reshape(SIDE * ROWS, HALF)

    def phase_one(b, copies):
        arrived(copies)

        def add(at, carry):
            got = sib_code[b, 1, at]
            acc[b, at] += decode(got, sib_scale.at[b, 1]).reshape(SIDE, ROWS, COLS)
            return carry

        lax.fori_loop(0, SIDE, add, 0)
        sent = []
        for step in (2, 1, 3):
            for axis in range(2):
                at = ((x, y)[axis] + step) % SIDE
                sent.append(
                    send_coded(
                        halves(b, axis, at), one_code.at[b, axis, step - 1],
                        one_scale.at[b, axis, step - 1], one_sem.at[b, axis, step - 1],
                        along(axis, step),
                    )
                )
        return sent

    def phase_two(b, copies):
        for axis in range(2):
            total = halves(b, axis, (x, y)[axis])
            for pair, step in zip(copies[axis::2], (2, 1, 3), strict=True):
                arrived(pair)
                total += decode(one_code[b, axis, step - 1, 1], one_scale.at[b, axis, step - 1, 1])
            part[b, axis] = total.reshape(SIDE, ROWS, HALF)
        sent = []
        for step in (2, 1, 3):
            for axis in range(2):
                at = ((y, x)[axis] + step) % SIDE
                sent.append(
                    send_coded(
                        part[b, axis, at], two_code.at[b, axis, step - 1],
                        two_scale.at[b, axis, step - 1], two_sem.at[b, axis, step - 1],
                        along(1 - axis, step),
                    )
                )
        return sent

    def plane_sum(b, copies):
        sides = []
        for axis in range(2):
            total = part[b, axis, (y, x)[axis]]
            for pair, step in zip(copies[axis::2], (2, 1, 3), strict=True):
                arrived(pair)
                total += decode(two_code[b, axis, step - 1, 1], two_scale.at[b, axis, step - 1, 1])
            sides.append(total)
        return jnp.concatenate(sides, axis=1)

    twin_0 = to_twin(0)
    own(0)
    twin_1 = to_twin(1)
    one_0 = phase_one(0, twin_0)
    own(1)
    one_1 = phase_one(1, twin_1)
    two_0 = phase_two(0, one_0)
    two_1 = phase_two(1, one_1)
    z_sum = send_coded(plane_sum(0, two_0), z_code, z_scale, z_sem, far)
    grad = plane_sum(1, two_1)
    for load in state:
        load.wait()
    arrived(z_sum)
    grad += decode(z_code[1], z_scale.at[1])
    piece, first_new, second_new = adamw(grad, par_buf[...], mom_buf[0], mom_buf[1])
    first_out[...] = first_new
    second_out[...] = second_new
    whole[inner, x, y] = piece

    def gather_one(block):
        at = block * 2 + core
        sent = []
        for step in (2, 1, 3):
            for axis in range(2):
                ref = whole.at[at, x, y, :, pl.ds(axis * HALF, HALF)]
                sent.append(send(ref, ref, up_sem.at[block, axis, step - 1], along(axis, step)))
        return sent

    def gather_two(block, copies):
        at = block * 2 + core
        sent, shared = [], []
        for axis in range(2):
            arrived(copies[axis::2])
            if axis == 0:
                ref = whole.at[at, :, y, :, pl.ds(0, HALF)]
            else:
                ref = whole.at[at, x, :, :, pl.ds(HALF, HALF)]
            for step in (2, 1, 3):
                sent.append(send(ref, ref, over_sem.at[block, axis, step - 1], along(1 - axis, step)))
            shared.append(send(ref, ref, twin_sem.at[block, axis, 3], twin))
        return sent, shared

    def gather_twin(block, copies):
        at = block * 2 + core
        shared = []
        for axis in range(2):
            for copy, step in zip(copies[3 * axis : 3 * axis + 3], (2, 1, 3), strict=True):
                copy.wait_recv()
                if axis == 0:
                    ref = whole.at[at, :, (y + SIDE - step) % SIDE, :, pl.ds(0, HALF)]
                else:
                    ref = whole.at[at, (x + SIDE - step) % SIDE, :, :, pl.ds(HALF, HALF)]
                shared.append(send(ref, ref, twin_sem.at[block, axis, step - 1], twin))
        return shared

    ref = whole.at[inner, x, y]
    far_piece = send(ref, ref, far_sem, far)
    up_0 = gather_one(plane)
    over_0, shared = gather_two(plane, up_0)
    arrived([far_piece])
    up_1 = gather_one(other)
    shared += gather_twin(plane, over_0)
    over_1, more = gather_two(other, up_1)
    shared += more
    shared += gather_twin(other, over_1)
    arrived(shared)
    store = pltpu.make_async_copy(whole, out, load_sem.at[8])
    store.start()
    for copy in started:
        copy.wait_send()
    store.wait()


def shards(activations, cotangent, tile_rows, params, first_moment, second_moment):
    rows, depth = activations.shape
    count = depth // BLOCK
    bf16, i16 = jnp.bfloat16, jnp.int16
    anywhere = pl.BlockSpec(memory_space=pl.ANY)
    vmem = pl.BlockSpec(memory_space=pltpu.VMEM)
    dma = pltpu.SemaphoreType.DMA
    whole, first_new, second_new = pl.pallas_call(
        kernel,
        out_shape=(
            jax.ShapeDtypeStruct((count, SIDE, SIDE, ROWS, COLS), bf16),
            jax.ShapeDtypeStruct((ROWS, COLS), F32),
            jax.ShapeDtypeStruct((ROWS, COLS), F32),
        ),
        in_specs=[
            anywhere, anywhere, pl.BlockSpec(memory_space=pltpu.SMEM), anywhere, anywhere, anywhere,
        ],
        out_specs=(anywhere, vmem, vmem),
        scratch_shapes=[
            pltpu.VMEM((4, rows, BLOCK), bf16),
            pltpu.VMEM((rows, COLS), bf16),
            pltpu.VMEM((rows, COLS), bf16),
            pltpu.VMEM((ROWS, COLS), bf16),
            pltpu.VMEM((2, ROWS, COLS), F32),
            pltpu.VMEM((2, SIDE, SIDE, ROWS, COLS), F32),
            pltpu.VMEM((BLOCK, COLS), F32),
            pltpu.VMEM((2, 2, SIDE, SIDE * ROWS, COLS), i16),
            pltpu.VMEM((2, 2, 8, LANES), F32),
            pltpu.VMEM((2, 2, 3, 2, SIDE * ROWS, HALF), i16),
            pltpu.VMEM((2, 2, 3, 2, 8, LANES), F32),
            pltpu.VMEM((2, 2, 3, 2, ROWS, HALF), i16),
            pltpu.VMEM((2, 2, 3, 2, 8, LANES), F32),
            pltpu.VMEM((2, ROWS, COLS), i16),
            pltpu.VMEM((2, 8, LANES), F32),
            pltpu.VMEM((2, 2, SIDE, ROWS, HALF), F32),
            pltpu.VMEM((count, SIDE, SIDE, ROWS, COLS), bf16),
            dma((9,)),
            dma((2, 2, 2)),
            dma((2, 2, 3, 2, 2)),
            dma((2, 2, 3, 2, 2)),
            dma((2, 2)),
            dma((2,)),
            dma((2, 2, 3, 2)),
            dma((2, 2, 3, 2)),
            dma((2, 2, 4, 2)),
        ],
        compiler_params=pltpu.CompilerParams(
            collective_id=0, has_side_effects=True, vmem_limit_bytes=56 * 2**20
        ),
    )(activations, cotangent, tile_rows, params, first_moment, second_moment)
    return whole.reshape(depth, COLS), first_new, second_new


def solution(mesh):
    in_specs = (
        P(("exp", "inner", "outer"), None),
        P(("exp", "inner", "outer"), None),
        P(("exp", "inner", "outer")),
        P(("exp", "inner"), None),
        P(("exp", "inner"), None),
        P(("exp", "inner"), None),
    )
    out_specs = (
        P("exp", None),
        P(("exp", "inner", "outer"), None),
        P(("exp", "inner", "outer"), None),
    )
    return jax.shard_map(shards, mesh=mesh, in_specs=in_specs, out_specs=out_specs, check_vma=False)
```

time: 298 us -> 62.4 us (0.21)
  waiting for transfers between devices: 257 us -> 0 us
  Pallas kernels: 0 us -> 56.6 us
  between operations: 13.8 us -> 0.66 us
  matrix products: 8.89 us -> 0 us
  local copies, waits for them, and re-layouts: 12.3 us -> 5.08 us
  other arithmetic: 5.37 us -> 0 us
    reduce_scatter x1 -> x0, waiting for transfers between devices: 111 us -> none  [shards(): lax.psum_scatter(lax.dot_general(activations, masked, (((0,), (0,)), ((),...]
    psum x1 -> x0, waiting for transfers between devices: 92.5 us -> none  [shards(): grad = lax.psum(partial_grad, 'outer')]
    pallas_call x0 -> x1, Pallas kernels: none -> 56.6 us  [shards(): pl.pallas_call(kernel, out_shape=(jax.ShapeDtypeStruct((count, SIDE, SIDE...]
    all_gather x1 -> x0, waiting for transfers between devices: 53.3 us -> none  [shards(): whole = lax.all_gather(row_shard, 'inner', axis=0, tiled=True)]
    dot_general x1 -> x0, matrix products: 8.89 us -> none  [shards(): lax.dot_general(activations, masked, (((0,), (0,)), ((), ())), preferred_...]
    unnamed x8 -> x7, local copies, waits for them, and re-layouts: 10.9 us -> 5.08 us
    convert_element_type x1 -> x0, other arithmetic: 4.64 us -> none  [adamw(): (weights - learn_rate * (update + weight_decay * weights)).astype(jnp.bfl...]
  transfers between devices with their start and end apart: 3 -> 0, of which waited for: 3 -> 0; matrix products, arithmetic and copies ran while one was open for 3% -> 0% of each run, Pallas kernels for 0% -> 0%
where the time goes in v1:
time: 62.4 us; the launch traced here: 62.3 us
  Pallas kernels  56.6 us (91%)
  local copies, waits for them, and re-layouts  5.08 us (8%)
  between operations  0.66 us (1%)
    pallas_call x1, Pallas kernels, shards(): pl.pallas_call(kernel, out_shape=(jax.ShapeDtypeStruct((count, SIDE, SIDE...  56.6 us
    unnamed x7, local copies, waits for them, and re-layouts  5.08 us

profile of v1, /device:TPU:1, one launch (start us, length us, event | category | flops | bytes accessed | tf_op | source)
XLA Modules:
  0.0 62.3 jit_solution(2834221870340862919)
XLA Ops:
  0.6 56.6 %shard_map.85 = (bf16[4,4,4,32,768]{4,3,2,1,0:T(8,128)(2,1)}, f32[32,768]{1,0:T(8,128)}, f32[32,768]{1,0:T(8,128)}) custom-call(bf16[1024,2048]{1,0:T(8,128)(2,1)} %acts.1, bf16[1024,768]{1,0:T(8,128)(2,1)} %cot.1, s32[8]{0:T(128)} %tiles.1, bf16[512,768]{1,0:T(8,128)(2,1)} %params.1, f32[512,768]{1,0:T(8,128)} %first.1, f32[512,768]{1,0:T(8,128)} %second.1), custom_call_target="tpu_custom_call" | custom-call | tf_op jit(solution)/shard_map/pallas_call | solution.py:294
  57.2 0.0 copy-start.1
  57.2 0.0 copy-start
  57.2 3.8 %copy.12 = bf16[2048,768]{1,0:T(8,128)(2,1)} copy(bf16[2048,768]{1,0:T(8,128)(2,1)} %bitcast.1) | data formatting | bytes 6291456
  61.0 0.0 copy-done.1
  61.0 0.6 %copy.13 = f32[32,768]{1,0:T(8,128)} copy(f32[32,768]{1,0:T(8,128)S(1)} %copy-done.1) | data formatting | bytes 196608
  61.7 0.0 copy-done
  61.7 0.6 %copy.14 = f32[32,768]{1,0:T(8,128)} copy(f32[32,768]{1,0:T(8,128)S(1)} %copy-done) | data formatting | bytes 196608
Async XLA Ops:
  57.2 3.8 %copy-start.1 = (f32[32,768]{1,0:T(8,128)S(1)}, f32[32,768]{1,0:T(8,128)}, u32[]{:S(2)}) copy-start(f32[32,768]{1,0:T(8,128)} %get-tuple-element.13) | copy-start | bytes 294916
  57.2 4.5 %copy-start = (f32[32,768]{1,0:T(8,128)S(1)}, f32[32,768]{1,0:T(8,128)}, u32[]{:S(2)}) copy-start(f32[32,768]{1,0:T(8,128)} %get-tuple-element.14) | copy-start | bytes 294916

commit v2 on v0

v2 whole, which is shorter than its diff:
```python
import functools

import jax
import jax.numpy as jnp
from jax import lax
from jax.experimental import pallas as pl
from jax.experimental.pallas import tpu as pltpu
from jax.sharding import PartitionSpec as P

beta_one = 0.9
beta_two = 0.95
learn_rate = 0.05
weight_decay = 0.1
epsilon = 1e-08

MESH = pl.DeviceIdType.MESH
SIDE = 4
ROWS = 32
COLS = 768
HALF = 384
GROUP = SIDE * ROWS
BLOCK = SIDE * GROUP
LANES = 128
LEVELS = 32767.0
PIECES = 8
F32 = jnp.float32


def adamw(grad, params, first_moment, second_moment):
    first_new = beta_one * first_moment + (1.0 - beta_one) * grad
    second_new = beta_two * second_moment + (1.0 - beta_two) * grad * grad
    update = (
        first_new / (1.0 - beta_one**3) / (jnp.sqrt(second_new / (1.0 - beta_two**3)) + epsilon)
    )
    weights = params.astype(F32)
    new_params = (weights - learn_rate * (update + weight_decay * weights)).astype(jnp.bfloat16)
    return (new_params, first_new, second_new)


def spread(row, columns):
    return jnp.concatenate([row] * (columns // LANES), axis=1)


def encode(value, code_ref, scale_ref):
    columns = value.shape[1]
    top = jnp.max(jnp.abs(value), axis=0, keepdims=True)
    peak = top[:, :LANES]
    for at in range(LANES, columns, LANES):
        peak = jnp.maximum(peak, top[:, at : at + LANES])
    peak = jnp.maximum(peak, 1e-30)
    code = jnp.round(value * spread(LEVELS / peak, columns)).astype(jnp.int32)
    code_ref[...] = code.astype(jnp.int16).reshape(code_ref.shape)
    scale_ref[...] = jnp.broadcast_to(peak * (1.0 / LEVELS), scale_ref.shape)


def decode(code, scale_ref):
    columns = code.shape[-1]
    value = code.reshape(-1, columns).astype(jnp.int32).astype(F32)
    return value * spread(scale_ref[0:1, :], columns)


def kernel(
    acts, cot, tiles, params, first, second,
    whole, first_out, second_out,
    act_buf, cot_buf, tile_buf, par_buf, mom_buf, acc, twin_half, part,
    one_code, two_code, z_code, scales, size,
    load_sem, sent_sem, sib_sem, one_sem, two_sem, z_sem, far_sem, up_sem, over_sem, twin_sem,
):
    exp, inner, outer = lax.axis_index("exp"), lax.axis_index("inner"), lax.axis_index("outer")
    place = (outer // SIDE, outer % SIDE)
    x, y = place
    plane, core = inner // 2, inner % 2
    other = 1 - plane

    twin = (exp, plane * 2 + 1 - core, outer)
    far = (exp, other * 2 + core, outer)

    def along(axis, step):
        if axis == 0:
            return (exp, inner, (x + step) % SIDE * SIDE + y)
        return (exp, inner, x * SIDE + (y + step) % SIDE)

    barrier = pltpu.get_barrier_semaphore()
    partners = [twin, far] + [along(a, s) for a in range(2) for s in (1, 2, 3)]
    for partner in partners:
        pl.semaphore_signal(barrier, inc=1, device_id=partner, device_id_type=MESH)

    blocks = (other, plane)

    def load_chunk(b, own):
        who = core if own else 1 - core
        at = pl.multiple_of((blocks[b] * 2 + who) * BLOCK, BLOCK)
        return pltpu.make_async_copy(
            acts.at[:, pl.ds(at, BLOCK)], act_buf.at[2 * b + own], load_sem.at[1 + 2 * b + own]
        )

    load_tiles = pltpu.make_async_copy(tiles, tile_buf, load_sem.at[8])
    load_cot = pltpu.make_async_copy(cot, cot_buf, load_sem.at[0])
    loads = [load_chunk(b, own) for b in range(2) for own in range(2)]
    mine = pl.ds(pl.multiple_of(outer * ROWS, ROWS), ROWS)
    state = [
        pltpu.make_async_copy(params.at[mine, :], par_buf, load_sem.at[5]),
        pltpu.make_async_copy(first.at[mine, :], mom_buf.at[0], load_sem.at[6]),
        pltpu.make_async_copy(second.at[mine, :], mom_buf.at[1], load_sem.at[7]),
    ]
    for load in [load_tiles, load_cot] + loads + state:
        load.start()

    load_tiles.wait()
    load_cot.wait()
    tile = cot_buf.shape[0] // tile_buf.shape[0]
    within = lax.broadcasted_iota(jnp.int32, (tile, COLS), 0)
    for t in range(tile_buf.shape[0]):
        rows = pl.ds(t * tile, tile)
        value = cot_buf[rows, :]
        cot_buf[rows, :] = jnp.where(within < tile_buf[t], value, jnp.zeros_like(value))

    def send(src, dst, send_sem, recv_sem, device):
        pltpu.make_async_remote_copy(
            src_ref=src, dst_ref=dst, send_sem=send_sem, recv_sem=recv_sem,
            device_id=device, device_id_type=MESH,
        ).start()

    def take(ref, sem):
        pltpu.make_async_copy(ref, ref, sem).wait()

    def send_coded(value, code, at, slot, sems, device):
        encode(value, code.at[(0,) + at], scales.at[0, slot])
        send(scales.at[0, slot], scales.at[1, slot], sent_sem.at[0], sems[1], device)
        send(code.at[(0,) + at], code.at[(1,) + at], sems[0], sems[1], device)

    def got(code, at, slot):
        return decode(code[(1,) + at], scales.at[1, slot])

    def product(at, pair):
        columns = pl.ds(pair * 2 * GROUP, 2 * GROUP)
        return lax.dot_general(
            act_buf[at, :, columns], cot_buf[...], (((0,), (0,)), ((), ())),
            preferred_element_type=F32,
        ).reshape(2, SIDE, ROWS, COLS)

    def to_twin(b):
        loads[2 * b].wait()
        for pair in range(2):
            acc[0, b, 2 * pair : 2 * pair + 2] = product(2 * b, pair)
            if b == 0 and pair == 0:
                pl.semaphore_wait(barrier, len(partners))
            xs = pl.ds(2 * pair, 2)
            send(acc.at[0, b, xs], twin_half.at[b, xs], sent_sem.at[1], sib_sem.at[b], twin)

    def own(b):
        loads[2 * b + 1].wait()
        for pair in range(2):
            acc[1, b, 2 * pair : 2 * pair + 2] = product(2 * b + 1, pair)

    def slab(ref, half, at):
        value = ref[at, :, :, :HALF] if half == 0 else ref[:, at, :, HALF:]
        return value.reshape(GROUP, HALF)

    def chip_sum(b, half, at):
        return slab(acc.at[1, b], half, at) + slab(twin_half.at[b], half, at)

    steps = (2, 1, 3)

    def slot_of(phase, b, half, step):
        return phase * 12 + b * 6 + half * 3 + step - 1

    def first_sends(b):
        take(twin_half.at[b], sib_sem.at[b])
        for step in steps:
            for half in range(2):
                value = chip_sum(b, half, (place[half] + step) % SIDE)
                send_coded(
                    value, one_code, (b, half, step - 1), slot_of(0, b, half, step),
                    (sent_sem.at[2], one_sem.at[b, half]), along(half, step),
                )

    def second_sends(b):
        for half in range(2):
            take(size, one_sem.at[b, half])
            value = chip_sum(b, half, place[half])
            for step in steps:
                value += got(one_code, (b, half, step - 1), slot_of(0, b, half, step))
            part[b, half] = value.reshape(SIDE, ROWS, HALF)
            for step in steps:
                send_coded(
                    part[b, half, (place[1 - half] + step) % SIDE], two_code,
                    (b, half, step - 1), slot_of(1, b, half, step),
                    (sent_sem.at[3], two_sem.at[b, half]), along(1 - half, step),
                )

    def plane_sum(b, half):
        take(size.at[pl.ds(0, 336), :], two_sem.at[b, half])
        total = part[b, half, place[1 - half]]
        for step in steps:
            total += got(two_code, (b, half, step - 1), slot_of(1, b, half, step))
        return total

    def far_sums():
        for half in range(2):
            send_coded(
                plane_sum(0, half), z_code, (half,), 24 + half,
                (sent_sem.at[4], z_sem.at[half]), far,
            )

    def columns(half):
        return pl.ds(half * HALF, HALF)

    def region(block, half, at):
        block = whole.at[block * 2 + core]
        if half == 0:
            return block.at[at, :, :, columns(half)]
        return block.at[:, at, :, columns(half)]

    def up(block, half):
        ref = whole.at[block * 2 + core, x, y, :, columns(half)]
        for step in steps:
            send(ref, ref, sent_sem.at[6], up_sem.at[block, half], along(1 - half, step))

    def step_adam(half):
        grad = plane_sum(1, half)
        take(size.at[pl.ds(0, 112), :], z_sem.at[half])
        grad += got(z_code, (half,), 24 + half)
        at = slice(half * HALF, (half + 1) * HALF)
        piece, first_new, second_new = adamw(
            grad, par_buf[:, at], mom_buf[0, :, at], mom_buf[1, :, at]
        )
        whole[inner, x, y, :, at] = piece
        ref = whole.at[inner, x, y, :, columns(half)]
        send(ref, ref, sent_sem.at[5], far_sem.at[half], far)
        up(plane, half)
        first_out[:, at] = first_new
        second_out[:, at] = second_new

    def gathered(block, half):
        take(whole.at[0, 0, pl.ds(0, 3), :, columns(0)], up_sem.at[block, half])

    def over(block, half, step):
        ref = region(block, half, place[half])
        send(ref, ref, sent_sem.at[7], over_sem.at[block, half, step - 1], along(half, step))

    def share(block, half, step):
        if step:
            take(whole.at[0, 0, pl.ds(0, 2)], over_sem.at[block, half, step - 1])
        ref = region(block, half, (place[half] + SIDE - step) % SIDE)
        send(ref, ref, sent_sem.at[8], twin_sem.at[0], twin)

    for b in range(2):
        to_twin(b)
        own(b)
    first_sends(0)
    first_sends(1)
    second_sends(0)
    second_sends(1)
    far_sums()
    for load in state:
        load.wait()
    for half in range(2):
        step_adam(half)
    for half in range(2):
        gathered(plane, half)
        over(plane, half, 1)
        over(plane, half, 3)
    for half in range(2):
        take(whole.at[0, 0, 0, :, columns(0)], far_sem.at[half])
        up(other, half)
    for half in range(2):
        over(plane, half, 2)
        share(plane, half, 0)
    for half in range(2):
        gathered(other, half)
        for step in steps:
            over(other, half, step)
    for half in range(2):
        share(other, half, 0)
        share(plane, half, 1)
        share(plane, half, 3)
    for half in range(2):
        share(plane, half, 2)
    for half in range(2):
        share(other, half, 1)
        share(other, half, 3)
    for half in range(2):
        share(other, half, 2)

    take(scales.at[0], sent_sem.at[0])
    take(acc.at[0], sent_sem.at[1])
    take(one_code.at[0], sent_sem.at[2])
    take(two_code.at[0], sent_sem.at[3])
    take(z_code.at[0], sent_sem.at[4])
    take(whole.at[0, 0, 0], sent_sem.at[5])
    take(whole.at[0, pl.ds(0, 3), pl.ds(0, 2)], sent_sem.at[6])
    take(whole.at[pl.ds(0, 3), pl.ds(0, 2)], sent_sem.at[7])
    take(whole.at[pl.ds(0, 2)], sent_sem.at[8])
    take(whole.at[pl.ds(0, 2)], twin_sem.at[0])


def hand_on(whole, first, second, out, first_out, second_out, sems):
    step = whole.shape[0] // PIECES
    copies = [
        pltpu.make_async_copy(first, first_out, sems.at[PIECES]),
        pltpu.make_async_copy(second, second_out, sems.at[PIECES + 1]),
    ]
    for i in range(PIECES):
        rows = pl.ds(i * step, step)
        copies.append(pltpu.make_async_copy(whole.at[rows, :], out.at[rows, :], sems.at[i]))
    for copy in copies:
        copy.start()
    for copy in copies:
        copy.wait()


def shards(activations, cotangent, tile_rows, params, first_moment, second_moment):
    rows, depth = activations.shape
    count = depth // BLOCK
    bf16, i16 = jnp.bfloat16, jnp.int16
    anywhere = pl.BlockSpec(memory_space=pltpu.HBM)
    vmem = pl.BlockSpec(memory_space=pltpu.VMEM)
    dma = pltpu.SemaphoreType.DMA
    whole, first_new, second_new = pl.pallas_call(
        kernel,
        out_shape=(
            pltpu.VMEM((count, SIDE, SIDE, ROWS, COLS), bf16),
            pltpu.VMEM((ROWS, COLS), F32),
            pltpu.VMEM((ROWS, COLS), F32),
        ),
        in_specs=[
            anywhere, anywhere, anywhere, anywhere, anywhere, anywhere,
        ],
        out_specs=(vmem, vmem, vmem),
        scratch_shapes=[
            pltpu.VMEM((4, rows, BLOCK), bf16),
            pltpu.VMEM((rows, COLS), bf16),
            pltpu.SMEM(tile_rows.shape, jnp.int32),
            pltpu.VMEM((ROWS, COLS), bf16),
            pltpu.VMEM((2, ROWS, COLS), F32),
            pltpu.VMEM((2, 2, SIDE, SIDE, ROWS, COLS), F32),
            pltpu.VMEM((2, SIDE, SIDE, ROWS, COLS), F32),
            pltpu.VMEM((2, 2, SIDE, ROWS, HALF), F32),
            pltpu.VMEM((2, 2, 2, 3, GROUP, HALF), i16),
            pltpu.VMEM((2, 2, 2, 3, ROWS, HALF), i16),
            pltpu.VMEM((2, 2, ROWS, HALF), i16),
            pltpu.VMEM((2, 26, 8, LANES), F32),
            pltpu.VMEM((1200, LANES), i16),
            dma((9,)),
            dma((9,)),
            dma((2,)),
            dma((2, 2)),
            dma((2, 2)),
            dma((2,)),
            dma((2,)),
            dma((2, 2)),
            dma((2, 2, 3)),
            dma((1,)),
        ],
        compiler_params=pltpu.CompilerParams(
            collective_id=0, has_side_effects=True, vmem_limit_bytes=58 * 2**20
        ),
    )(activations, cotangent, tile_rows, params, first_moment, second_moment)
    whole = whole.reshape(depth, COLS)
    return pl.pallas_call(
        hand_on,
        out_shape=tuple(jax.ShapeDtypeStruct(a.shape, a.dtype) for a in (whole, first_new, second_new)),
        in_specs=[pl.BlockSpec(memory_space=pl.ANY)] * 3,
        out_specs=(anywhere,) * 3,
        scratch_shapes=[dma((PIECES + 2,))],
        compiler_params=pltpu.CompilerParams(vmem_limit_bytes=4 * 2**20),
    )(whole, first_new, second_new)


def solution(mesh):
    in_specs = (
        P(("exp", "inner", "outer"), None),
        P(("exp", "inner", "outer"), None),
        P(("exp", "inner", "outer")),
        P(("exp", "inner"), None),
        P(("exp", "inner"), None),
        P(("exp", "inner"), None),
    )
    out_specs = (
        P("exp", None),
        P(("exp", "inner", "outer"), None),
        P(("exp", "inner", "outer"), None),
    )
    return jax.shard_map(shards, mesh=mesh, in_specs=in_specs, out_specs=out_specs, check_vma=False)
```

time: 298 us -> 53.3 us (0.18)
  waiting for transfers between devices: 257 us -> 0 us
  Pallas kernels: 0 us -> 52.1 us
  between operations: 13.8 us -> 0.64 us
  local copies, waits for them, and re-layouts: 12.3 us -> 0 us
  matrix products: 8.89 us -> 0 us
  other arithmetic: 5.37 us -> 0 us
    reduce_scatter x1 -> x0, waiting for transfers between devices: 111 us -> none  [shards(): lax.psum_scatter(lax.dot_general(activations, masked, (((0,), (0,)), ((),...]
    psum x1 -> x0, waiting for transfers between devices: 92.5 us -> none  [shards(): grad = lax.psum(partial_grad, 'outer')]
    all_gather x1 -> x0, waiting for transfers between devices: 53.3 us -> none  [shards(): whole = lax.all_gather(row_shard, 'inner', axis=0, tiled=True)]
    pallas_call x0 -> x2, Pallas kernels: none -> 52.1 us  [the longest x1 50.3 us: shards(): pl.pallas_call(kernel, out_shape=(pltpu.VMEM((count, SIDE, SIDE, ROWS, CO...]
    unnamed x8 -> x0, local copies, waits for them, and re-layouts: 10.9 us -> none
    dot_general x1 -> x0, matrix products: 8.89 us -> none  [shards(): lax.dot_general(activations, masked, (((0,), (0,)), ((), ())), preferred_...]
    convert_element_type x1 -> x0, other arithmetic: 4.64 us -> none  [adamw(): (weights - learn_rate * (update + weight_decay * weights)).astype(jnp.bfl...]
  transfers between devices with their start and end apart: 3 -> 0, of which waited for: 3 -> 0; matrix products, arithmetic and copies ran while one was open for 3% -> 0% of each run, Pallas kernels for 0% -> 0%
where the time goes in v2:
time: 53.3 us; the launch traced here: 52.8 us
  Pallas kernels  52.1 us (98%)
  between operations  0.64 us (1%)
    pallas_call x1, Pallas kernels, shards(): pl.pallas_call(kernel, out_shape=(pltpu.VMEM((count, SIDE, SIDE, ROWS, CO...  50.3 us
    pallas_call x1, Pallas kernels, shards(): pl.pallas_call(hand_on, out_shape=tuple((jax.ShapeDtypeStruct(a.shape, a....  1.8 us

profile of v2, /device:TPU:1, one launch (start us, length us, event | category | flops | bytes accessed | tf_op | source)
XLA Modules:
  0.0 52.8 jit_solution(2285598257380085510)
XLA Ops:
  0.6 50.3 %shard_map.85 = (bf16[4,4,4,32,768]{4,3,2,1,0:T(8,128)(2,1)S(1)}, f32[32,768]{1,0:T(8,128)S(1)}, f32[32,768]{1,0:T(8,128)S(1)}) custom-call(bf16[1024,2048]{1,0:T(8,128)(2,1)} %acts.1, bf16[1024,768]{1,0:T(8,128)(2,1)} %cot.1, s32[8]{0:T(128)} %tiles.1, bf16[512,768]{1,0:T(8,128)(2,1)} %params.1, f32[512,768]{1,0:T(8,128)} %first.1, f32[512,768]{1,0:T(8,128)} %second.1), custom_call_target="tpu_custom_call" | custom-call | tf_op jit(solution)/shard_map/pallas_call | solution.py:320
  51.0 1.8 %shard_map.86 = (bf16[2048,768]{1,0:T(8,128)(2,1)}, f32[32,768]{1,0:T(8,128)}, f32[32,768]{1,0:T(8,128)}) custom-call(bf16[2048,768]{1,0:T(8,128)(2,1)S(1)} %bitcast.1, f32[32,768]{1,0:T(8,128)S(1)} %get-tuple-element.7.first, f32[32,768]{1,0:T(8,128)S(1)} %get-tuple-element.8.second), custom_call_target="tpu_custom_call" | custom-call | tf_op jit(solution)/shard_map/pallas_call | solution.py:361

commit v3 on v2

--- a/solution.py
+++ b/solution.py
@@ -22,7 +22,7 @@
 BLOCK = SIDE * GROUP
 LANES = 128
 LEVELS = 32767.0
-PIECES = 8
+PIECES = 16
 F32 = jnp.float32
 
 
@@ -103,11 +103,13 @@
         pltpu.make_async_copy(first.at[mine, :], mom_buf.at[0], load_sem.at[6]),
         pltpu.make_async_copy(second.at[mine, :], mom_buf.at[1], load_sem.at[7]),
     ]
-    for load in [load_tiles, load_cot] + loads + state:
+    for load in [load_tiles, load_cot, loads[0]]:
         load.start()
 
     load_tiles.wait()
     load_cot.wait()
+    for load in loads[1:] + state:
+        load.start()
     tile = cot_buf.shape[0] // tile_buf.shape[0]
     within = lax.broadcasted_iota(jnp.int32, (tile, COLS), 0)
     for t in range(tile_buf.shape[0]):
@@ -139,14 +141,18 @@
             preferred_element_type=F32,
         ).reshape(2, SIDE, ROWS, COLS)
 
-    def to_twin(b):
+    def to_twin(b, pair):
+        xs = pl.ds(2 * pair, 2)
+        send(acc.at[0, b, xs], twin_half.at[b, xs], sent_sem.at[1], sib_sem.at[b], twin)
+
+    def others(b):
         loads[2 * b].wait()
         for pair in range(2):
             acc[0, b, 2 * pair : 2 * pair + 2] = product(2 * b, pair)
-            if b == 0 and pair == 0:
-                pl.semaphore_wait(barrier, len(partners))
-            xs = pl.ds(2 * pair, 2)
-            send(acc.at[0, b, xs], twin_half.at[b, xs], sent_sem.at[1], sib_sem.at[b], twin)
+            if b == 0:
+                if pair == 0:
+                    pl.semaphore_wait(barrier, len(partners))
+                to_twin(b, pair)
 
     def own(b):
         loads[2 * b + 1].wait()
@@ -160,13 +166,12 @@
     def chip_sum(b, half, at):
         return slab(acc.at[1, b], half, at) + slab(twin_half.at[b], half, at)
 
-    steps = (2, 1, 3)
+    steps = (1, 3, 2)
 
     def slot_of(phase, b, half, step):
         return phase * 12 + b * 6 + half * 3 + step - 1
 
     def first_sends(b):
-        take(twin_half.at[b], sib_sem.at[b])
         for step in steps:
             for half in range(2):
                 value = chip_sum(b, half, (place[half] + step) % SIDE)
@@ -215,7 +220,16 @@
     def up(block, half):
         ref = whole.at[block * 2 + core, x, y, :, columns(half)]
         for step in steps:
-            send(ref, ref, sent_sem.at[6], up_sem.at[block, half], along(1 - half, step))
+            send(ref, ref, sent_sem.at[6], up_sem.at[block, half, step - 1], along(1 - half, step))
+
+    def over(block, half, piece, some=steps):
+        if piece:
+            take(whole.at[0, 0, 0, :, columns(0)], up_sem.at[block, half, piece - 1])
+        at = (place[1 - half] + SIDE - piece) % SIDE
+        row, col = (x, at) if half == 0 else (at, y)
+        ref = whole.at[block * 2 + core, row, col, :, columns(half)]
+        for step in some:
+            send(ref, ref, sent_sem.at[7], over_sem.at[block, half, step - 1], along(half, step))
 
     def step_adam(half):
         grad = plane_sum(1, half)
@@ -232,49 +246,59 @@
         first_out[:, at] = first_new
         second_out[:, at] = second_new
 
-    def gathered(block, half):
-        take(whole.at[0, 0, pl.ds(0, 3), :, columns(0)], up_sem.at[block, half])
-
-    def over(block, half, step):
-        ref = region(block, half, place[half])
-        send(ref, ref, sent_sem.at[7], over_sem.at[block, half, step - 1], along(half, step))
-
-    def share(block, half, step):
-        if step:
+    def relay(half):
+        for way, step in enumerate((1, 3)):
+            take(whole.at[0, 0, pl.ds(0, 2)], over_sem.at[plane, half, step - 1])
+            at, some = (place[half] + SIDE - step) % SIDE, pl.ds(2 * way, 2)
+            block = whole.at[inner]
+            if half == 0:
+                ref = block.at[at, some, :, columns(half)]
+            else:
+                ref = block.at[some, at, :, columns(half)]
+            send(ref, ref, sent_sem.at[7], over_sem.at[plane, half, 1], along(half, step))
+
+    def share(block, half, step, here=False):
+        if step and not here:
             take(whole.at[0, 0, pl.ds(0, 2)], over_sem.at[block, half, step - 1])
         ref = region(block, half, (place[half] + SIDE - step) % SIDE)
         send(ref, ref, sent_sem.at[8], twin_sem.at[0], twin)
 
     for b in range(2):
-        to_twin(b)
+        others(b)
         own(b)
+    take(twin_half.at[0], sib_sem.at[0])
+    to_twin(1, 0)
+    to_twin(1, 1)
     first_sends(0)
+    take(twin_half.at[1], sib_sem.at[1])
     first_sends(1)
     second_sends(0)
+    far_sums()
     second_sends(1)
-    far_sums()
     for load in state:
         load.wait()
     for half in range(2):
         step_adam(half)
     for half in range(2):
-        gathered(plane, half)
-        over(plane, half, 1)
-        over(plane, half, 3)
+        over(plane, half, 0, (1, 3))
+    for piece in (1, 3, 2):
+        for half in range(2):
+            over(plane, half, piece, (1, 3))
     for half in range(2):
         take(whole.at[0, 0, 0, :, columns(0)], far_sem.at[half])
         up(other, half)
-    for half in range(2):
-        over(plane, half, 2)
+        over(other, half, 0)
+    for half in range(2):
+        relay(half)
+    for half in range(2):
         share(plane, half, 0)
-    for half in range(2):
-        gathered(other, half)
-        for step in steps:
-            over(other, half, step)
+    for piece in (1, 3, 2):
+        for half in range(2):
+            over(other, half, piece)
     for half in range(2):
         share(other, half, 0)
-        share(plane, half, 1)
-        share(plane, half, 3)
+        share(plane, half, 1, True)
+        share(plane, half, 3, True)
     for half in range(2):
         share(plane, half, 2)
     for half in range(2):
@@ -349,7 +373,7 @@
             dma((2, 2)),
             dma((2,)),
             dma((2,)),
-            dma((2, 2)),
+            dma((2, 2, 3)),
             dma((2, 2, 3)),
             dma((1,)),
         ],

time: 53.3 us -> 50.7 us (0.951)
  Pallas kernels: 52.1 us -> 50 us
    pallas_call x1, Pallas kernels: 50.3 us -> 48.1 us  [shards(): pl.pallas_call(kernel, out_shape=(pltpu.VMEM((count, SIDE, SIDE, ROWS, CO...]
where the time goes in v3:
time: 50.7 us; the launch traced here: 50.6 us
  Pallas kernels  50 us (99%)
  between operations  0.64 us (1%)
    pallas_call x1, Pallas kernels, shards(): pl.pallas_call(kernel, out_shape=(pltpu.VMEM((count, SIDE, SIDE, ROWS, CO...  48.1 us
    pallas_call x1, Pallas kernels, shards(): pl.pallas_call(hand_on, out_shape=tuple((jax.ShapeDtypeStruct(a.shape, a....  1.87 us

profile of v3, /device:TPU:1, one launch (start us, length us, event | category | flops | bytes accessed | tf_op | source)
XLA Modules:
  0.0 50.6 jit_solution(15104022054892657870)
XLA Ops:
  0.6 48.1 %shard_map.85 = (bf16[4,4,4,32,768]{4,3,2,1,0:T(8,128)(2,1)S(1)}, f32[32,768]{1,0:T(8,128)S(1)}, f32[32,768]{1,0:T(8,128)S(1)}) custom-call(bf16[1024,2048]{1,0:T(8,128)(2,1)} %acts.1, bf16[1024,768]{1,0:T(8,128)(2,1)} %cot.1, s32[8]{0:T(128)} %tiles.1, bf16[512,768]{1,0:T(8,128)(2,1)} %params.1, f32[512,768]{1,0:T(8,128)} %first.1, f32[512,768]{1,0:T(8,128)} %second.1), custom_call_target="tpu_custom_call" | custom-call | tf_op jit(solution)/shard_map/pallas_call | solution.py:344
  48.8 1.9 %shard_map.86 = (bf16[2048,768]{1,0:T(8,128)(2,1)}, f32[32,768]{1,0:T(8,128)}, f32[32,768]{1,0:T(8,128)}) custom-call(bf16[2048,768]{1,0:T(8,128)(2,1)S(1)} %bitcast.1, f32[32,768]{1,0:T(8,128)S(1)} %get-tuple-element.7.first, f32[32,768]{1,0:T(8,128)S(1)} %get-tuple-element.8.second), custom_call_target="tpu_custom_call" | custom-call | tf_op jit(solution)/shard_map/pallas_call | solution.py:385

commit v4 on v3

--- a/solution.py
+++ b/solution.py
@@ -180,23 +180,29 @@
                     (sent_sem.at[2], one_sem.at[b, half]), along(half, step),
                 )
 
+    def chip_piece(b, half, second):
+        row, col = (x, second) if half == 0 else (second, y)
+        cols = slice(half * HALF, (half + 1) * HALF)
+        value = acc[1, b, row, col, :, cols] + twin_half[b, row, col, :, cols]
+        for step in steps:
+            value += got(one_code, (b, half, step - 1, second), slot_of(0, b, half, step))
+        return value
+
     def second_sends(b):
         for half in range(2):
             take(size, one_sem.at[b, half])
-            value = chip_sum(b, half, place[half])
-            for step in steps:
-                value += got(one_code, (b, half, step - 1), slot_of(0, b, half, step))
-            part[b, half] = value.reshape(SIDE, ROWS, HALF)
             for step in steps:
                 send_coded(
-                    part[b, half, (place[1 - half] + step) % SIDE], two_code,
+                    chip_piece(b, half, (place[1 - half] + step) % SIDE), two_code,
                     (b, half, step - 1), slot_of(1, b, half, step),
                     (sent_sem.at[3], two_sem.at[b, half]), along(1 - half, step),
                 )
+        for half in range(2):
+            part[b, half] = chip_piece(b, half, place[1 - half])
 
     def plane_sum(b, half):
         take(size.at[pl.ds(0, 336), :], two_sem.at[b, half])
-        total = part[b, half, place[1 - half]]
+        total = part[b, half]
         for step in steps:
             total += got(two_code, (b, half, step - 1), slot_of(1, b, half, step))
         return total
@@ -229,7 +235,8 @@
         row, col = (x, at) if half == 0 else (at, y)
         ref = whole.at[block * 2 + core, row, col, :, columns(half)]
         for step in some:
-            send(ref, ref, sent_sem.at[7], over_sem.at[block, half, step - 1], along(half, step))
+            sem = over_sem.at[block, half, step - 1, 0 if piece < 2 else 1]
+            send(ref, ref, sent_sem.at[7], sem, along(half, step))
 
     def step_adam(half):
         grad = plane_sum(1, half)
@@ -246,20 +253,34 @@
         first_out[:, at] = first_new
         second_out[:, at] = second_new
 
+    def landed(block, half, step, group):
+        take(whole.at[0, 0, 0], over_sem.at[block, half, step - 1, group])
+
+    def share_group(half, step, group):
+        landed(other, half, step, group)
+        at = (place[half] + SIDE - step) % SIDE
+        for piece in ((0, 1), (3, 2))[group]:
+            second = (place[1 - half] + SIDE - piece) % SIDE
+            row, col = (at, second) if half == 0 else (second, at)
+            ref = whole.at[other * 2 + core, row, col, :, columns(half)]
+            send(ref, ref, sent_sem.at[8], twin_sem.at[0], twin)
+
     def relay(half):
         for way, step in enumerate((1, 3)):
-            take(whole.at[0, 0, pl.ds(0, 2)], over_sem.at[plane, half, step - 1])
+            landed(plane, half, step, 0)
+            landed(plane, half, step, 1)
             at, some = (place[half] + SIDE - step) % SIDE, pl.ds(2 * way, 2)
             block = whole.at[inner]
             if half == 0:
                 ref = block.at[at, some, :, columns(half)]
             else:
                 ref = block.at[some, at, :, columns(half)]
-            send(ref, ref, sent_sem.at[7], over_sem.at[plane, half, 1], along(half, step))
+            send(ref, ref, sent_sem.at[7], over_sem.at[plane, half, 1, way], along(half, step))
 
     def share(block, half, step, here=False):
         if step and not here:
-            take(whole.at[0, 0, pl.ds(0, 2)], over_sem.at[block, half, step - 1])
+            landed(block, half, step, 0)
+            landed(block, half, step, 1)
         ref = region(block, half, (place[half] + SIDE - step) % SIDE)
         send(ref, ref, sent_sem.at[8], twin_sem.at[0], twin)
 
@@ -290,6 +311,8 @@
         over(other, half, 0)
     for half in range(2):
         relay(half)
+        share(plane, half, 1, True)
+        share(plane, half, 3, True)
     for half in range(2):
         share(plane, half, 0)
     for piece in (1, 3, 2):
@@ -297,15 +320,12 @@
             over(other, half, piece)
     for half in range(2):
         share(other, half, 0)
-        share(plane, half, 1, True)
-        share(plane, half, 3, True)
     for half in range(2):
         share(plane, half, 2)
-    for half in range(2):
-        share(other, half, 1)
-        share(other, half, 3)
-    for half in range(2):
-        share(other, half, 2)
+    for group in range(2):
+        for step in steps:
+            for half in range(2):
+                share_group(half, step, group)
 
     take(scales.at[0], sent_sem.at[0])
     take(acc.at[0], sent_sem.at[1])
@@ -360,8 +380,8 @@
             pltpu.VMEM((2, ROWS, COLS), F32),
             pltpu.VMEM((2, 2, SIDE, SIDE, ROWS, COLS), F32),
             pltpu.VMEM((2, SIDE, SIDE, ROWS, COLS), F32),
-            pltpu.VMEM((2, 2, SIDE, ROWS, HALF), F32),
-            pltpu.VMEM((2, 2, 2, 3, GROUP, HALF), i16),
+            pltpu.VMEM((2, 2, ROWS, HALF), F32),
+            pltpu.VMEM((2, 2, 2, 3, SIDE, ROWS, HALF), i16),
             pltpu.VMEM((2, 2, 2, 3, ROWS, HALF), i16),
             pltpu.VMEM((2, 2, ROWS, HALF), i16),
             pltpu.VMEM((2, 26, 8, LANES), F32),
@@ -374,7 +394,7 @@
             dma((2,)),
             dma((2,)),
             dma((2, 2, 3)),
-            dma((2, 2, 3)),
+            dma((2, 2, 3, 2)),
             dma((1,)),
         ],
         compiler_params=pltpu.CompilerParams(

time: 50.7 us -> 50.8 us (level)
  no operation moved by 1% of the time
where the time goes in v4:
time: 50.8 us; the launch traced here: 50.7 us
  Pallas kernels  50 us (98%)
  between operations  0.64 us (1%)
    pallas_call x1, Pallas kernels, shards(): pl.pallas_call(kernel, out_shape=(pltpu.VMEM((count, SIDE, SIDE, ROWS, CO...  48.2 us
    pallas_call x1, Pallas kernels, shards(): pl.pallas_call(hand_on, out_shape=tuple((jax.ShapeDtypeStruct(a.shape, a....  1.87 us

profile of v4, /device:TPU:1, one launch (start us, length us, event | category | flops | bytes accessed | tf_op | source)
XLA Modules:
  0.0 50.7 jit_solution(803385719134259078)
XLA Ops:
  0.6 48.2 %shard_map.85 = (bf16[4,4,4,32,768]{4,3,2,1,0:T(8,128)(2,1)S(1)}, f32[32,768]{1,0:T(8,128)S(1)}, f32[32,768]{1,0:T(8,128)S(1)}) custom-call(bf16[1024,2048]{1,0:T(8,128)(2,1)} %acts.1, bf16[1024,768]{1,0:T(8,128)(2,1)} %cot.1, s32[8]{0:T(128)} %tiles.1, bf16[512,768]{1,0:T(8,128)(2,1)} %params.1, f32[512,768]{1,0:T(8,128)} %first.1, f32[512,768]{1,0:T(8,128)} %second.1), custom_call_target="tpu_custom_call" | custom-call | tf_op jit(solution)/shard_map/pallas_call | solution.py:364
  48.8 1.9 %shard_map.86 = (bf16[2048,768]{1,0:T(8,128)(2,1)}, f32[32,768]{1,0:T(8,128)}, f32[32,768]{1,0:T(8,128)}) custom-call(bf16[2048,768]{1,0:T(8,128)(2,1)S(1)} %bitcast.1, f32[32,768]{1,0:T(8,128)S(1)} %get-tuple-element.7.first, f32[32,768]{1,0:T(8,128)S(1)} %get-tuple-element.8.second), custom_call_target="tpu_custom_call" | custom-call | tf_op jit(solution)/shard_map/pallas_call | solution.py:405
